TPU v7x, 256 devices: a whole 4x4x8 slice. The times are simulated.
256 devices in a mesh: region: 32 (over z, x), cols: 8 (over y, core).
Axes of the slice: x: 4, y: 4, z: 8, core: 2. Of those that a mesh axis runs over, the one named last changes fastest.
Arguments:
- innovations: float32 [32, 262144], P('cols', 'region'), may hold values from -6 to 6
- coords: float32 [3, 262144], P(None, 'region'), may hold values from -1 to 1, as said below
- background_std: float32 [262144], P('region'), may hold values from 0.3 to 1.2
- obs_variance: float32 [262144], P('region'), may hold values from 0.25 to 1
- block_count: int32 [1024], P('region'), may hold values from 128 to 256, as said below
- pair_list: int32 [2, 24576], P(None, ('region', 'cols')), may hold values from 0 to 54, as said below
- pair_count: int32 [256], P(('region', 'cols')), may hold values from 4 to 96, as said below
Outputs:
- solution_field: float32 [32, 262144], P('cols', 'region')
- residual: float32 [32, 262144], P('cols', 'region')
Inputs may be any that keep to these rules, and one draw needn't show every extreme that they name: `coords`: every column is a unit vector. `block_count`: the first block of every region holds 256 live observations. `pair_list`: live entries of a device come first in its 96 slots; row 0 names a block whose index within the region lies among the device's own 32 // (devices on cols) blocks (the device at cols position c owns blocks c * that many onward), row 1 is at least row 0 and at most row 23, and the partner block exists; no unordered pair appears twice; dead slots hold 0. `pair_count`: some device has all 96 slots live.
All inputs are finite; a program needn't handle non-finite values.
Results may differ from a plain program's by a relative error of at most 0.0003.
Values sent between devices are 32-bit elements; how exact they have to be, the bound alone decides.
No kernel may reach another device: no remote copies, remote signals or barrier semaphores. Data moves between devices by JAX's collectives and lax.ppermute only.
A program may use at most 64 MiB of HBM per device.

v0:
```python
import functools

import jax
import jax.numpy as jnp
from jax import lax
from jax.experimental import pallas as pl
from jax.experimental.pallas import tpu as pltpu
from jax.sharding import PartitionSpec as P

BLOCK = 256
KMAX = 23
SUPPORT = 1000.0 / 6371.0

STRETCH = 4.0**0.2
TOP = 5.0 / STRETCH**4
GAMMA = 2.0 * STRETCH**2 / SUPPORT**2
FAR = 2.0**100

ROWS = 32
CHIP = 8 * BLOCK
HALF = 4 * BLOCK
WIDE = CHIP + 128
AXES = ("region", "cols")

bf16 = jnp.bfloat16
f32 = jnp.float32


def dot(a, b):
    return jnp.dot(a, b, preferred_element_type=f32)


def two_parts(x):
    high = x.astype(bf16)
    return high, (x - high.astype(f32)).astype(bf16)


def three_parts(x):
    first = x.astype(bf16).astype(f32)
    rest = x - first
    second = rest.astype(bf16).astype(f32)
    return first, second, (rest - second).astype(bf16).astype(f32)


def vmem(count):
    return [pl.BlockSpec(memory_space=pltpu.VMEM)] * count


def smem(count):
    return [pl.BlockSpec(memory_space=pltpu.SMEM)] * count


def hbm(count):
    return [pl.BlockSpec(memory_space=pltpu.HBM)] * count


def in_hbm(array):
    return pltpu.with_memory_space_constraint(array, pltpu.HBM)


def params(mebibytes):
    return pltpu.CompilerParams(vmem_limit_bytes=mebibytes * 1024 * 1024)


def chip_at(place, row_at):
    turned = row_at ^ (2 * place[3])
    return turned ^ (turned >> 1)


def split_kernel(
    place, count, pairs, innovations, own, ahead1, ahead2, ahead3, held, sems
):
    copies = [pltpu.make_async_copy(pairs, held, sems.at[4])]
    outs = (own, ahead1, ahead2, ahead3)
    for step, out in enumerate(outs):
        at = chip_at(place, (place[2] + step) & 3) * CHIP
        source = innovations.at[:, pl.ds(pl.multiple_of(at, CHIP), CHIP)]
        copies.append(
            pltpu.make_async_copy(source, out.at[:, pl.ds(0, CHIP)], sems.at[step])
        )
    for copy in copies:
        copy.start()
    copies[0].wait()
    left, right = held[0:1, :], held[1:2, :]
    slot = lax.broadcasted_iota(jnp.int32, left.shape, 1)
    live = jnp.where(slot < count[0], left * 24 + (right - left), -1).astype(f32)
    for copy in copies[1:]:
        copy.wait()
    for out in outs:
        out[:, CHIP:] = jnp.full((4, 128), -1.0, f32)
        out[0:1, CHIP : CHIP + live.shape[1]] = live


def split(place, count, pairs, innovations):
    part = jax.ShapeDtypeStruct((4, WIDE), f32)
    return pl.pallas_call(
        split_kernel,
        out_shape=(part, part, part, part),
        in_specs=smem(2) + hbm(2),
        out_specs=vmem(4),
        scratch_shapes=[
            pltpu.VMEM(pairs.shape, jnp.int32),
            pltpu.SemaphoreType.DMA((5,)),
        ],
        compiler_params=params(4),
        name="split",
    )(place, count, in_hbm(pairs), in_hbm(innovations))


def assemble_kernel(place, own, behind1, behind2, behind3, out):
    for y in range(4):
        step = (place[2] - y) & 3
        value = jnp.where(step == 0, own[...], behind1[...])
        value = jnp.where(step == 2, behind2[...], value)
        value = jnp.where(step == 3, behind3[...], value)
        out[4 * y : 4 * y + 4, :] = value


def assemble(place, own, behind1, behind2, behind3):
    return pl.pallas_call(
        assemble_kernel,
        out_shape=jax.ShapeDtypeStruct((16, WIDE), f32),
        in_specs=smem(1) + vmem(4),
        out_specs=vmem(1)[0],
        compiler_params=params(4),
        name="assemble",
    )(place, own, behind1, behind2, behind3)


def pair_flags(row_at, core, mine, other):
    sub = lax.broadcasted_iota(jnp.int32, (8, 128), 0)
    col = lax.broadcasted_iota(jnp.int32, (8, 128), 1)
    far = col < 24
    near = col - lax.div(col, 8) * 8
    ahead = 8 * (lax.div(col, 8) + 1)
    offset = jnp.where(far, ahead + sub - near, jnp.abs(near - sub))
    left_up = jnp.where(far, near, jnp.minimum(near, sub))
    left_down = jnp.where(far, 7 - sub, 7 - jnp.maximum(near, sub))
    left = jnp.where(core == 0, left_up, left_down)
    valid = (offset >= 0) & (offset <= KMAX) & (col < 32)
    target = jnp.where(valid, (row_at * 8 + left) * 24 + offset, -7).astype(f32)
    hit = jnp.zeros((8, 128), f32)
    for source in (mine, other):
        known = source[0:1, CHIP:]
        for y in (1, 2, 3):
            known = jnp.where(row_at == y, source[4 * y : 4 * y + 1, CHIP:], known)
        for i in range(96):
            code = jnp.broadcast_to(known[0:1, i : i + 1], (8, 128))
            hit = jnp.where(code == target, 1.0, hit)
    return jnp.where(hit > 0.5, 0.0, FAR)


def points_kernel(
    place,
    all_counts,
    all_coords,
    all_std,
    all_variance,
    base,
    aux,
    first,
    right,
    coords,
    std,
    variance,
    counts,
    sems,
):
    row_at, core = place[0], place[1]
    chip = pl.ds(pl.multiple_of(row_at * CHIP, CHIP), CHIP)
    copies = [
        pltpu.make_async_copy(source.at[:, chip], to, sems.at[i])
        for i, (source, to) in enumerate(
            ((all_coords, coords), (all_std, std), (all_variance, variance))
        )
    ]
    copies.append(pltpu.make_async_copy(all_counts, counts, sems.at[3]))
    for copy in copies:
        copy.start()
    base[...] = jnp.zeros((8, CHIP), f32)
    for copy in copies:
        copy.wait()
    lane = lax.broadcasted_iota(jnp.int32, (1, BLOCK), 1)
    for j in range(8):
        source = j + core * (7 - 2 * j)
        here = slice(j * BLOCK, (j + 1) * BLOCK)
        region = pl.ds(pl.multiple_of(source * BLOCK, BLOCK), BLOCK)
        live = (lane < counts[row_at * 8 + source]).astype(f32)
        base[0:3, here] = coords[:, region]
        aux[0:1, here] = std[0:1, region] * live
        aux[1:2, here] = variance[0:1, region]
    sub = lax.broadcasted_iota(jnp.int32, (8, CHIP), 0)
    points = base[...]
    side = jnp.where(sub < 3, points * (-GAMMA), jnp.where(sub == 3, GAMMA, 0.0))
    a1, a2, a3 = three_parts(side)
    first[...] = a1
    right[0:16, :] = jnp.concatenate([a2, a2], 0).astype(bf16)
    right[16:32, :] = jnp.concatenate([a1, a3], 0).astype(bf16)


def points(place, counts, coords, std, variance):
    return pl.pallas_call(
        points_kernel,
        out_shape=(
            jax.ShapeDtypeStruct((8, CHIP), f32),
            jax.ShapeDtypeStruct((8, CHIP), f32),
            jax.ShapeDtypeStruct((8, CHIP), f32),
            jax.ShapeDtypeStruct((32, CHIP), bf16),
        ),
        in_specs=smem(1) + hbm(4),
        out_specs=vmem(4),
        scratch_shapes=[
            pltpu.VMEM((3, CHIP), f32),
            pltpu.VMEM((1, CHIP), f32),
            pltpu.VMEM((1, CHIP), f32),
            pltpu.SMEM(counts.shape, jnp.int32),
            pltpu.SemaphoreType.DMA((4,)),
        ],
        compiler_params=params(4),
        name="points",
    )(place, in_hbm(counts), in_hbm(coords), in_hbm(std), in_hbm(variance))


def vectors_kernel(place, mine, other, base, aux, halo, vector, flags):
    core = place[1]
    pairs = pair_flags(place[0], core, mine, other)
    flags[...] = pairs
    halo[32:40, 0:CHIP] = base[...]
    halo[32:40, CHIP:] = pairs
    halo[0:32, CHIP:] = jnp.zeros((32, 128), f32)
    for j in range(8):
        here = slice(j * BLOCK, (j + 1) * BLOCK)
        source = (j + core * (7 - 2 * j)) * BLOCK
        local = pl.ds(pl.multiple_of(source, BLOCK), BLOCK)
        spread = aux[0:1, here]
        got, had = other[:, local], mine[:, local]
        for y in range(4):
            rows = slice(4 * y, 4 * y + 4)
            up = jnp.concatenate([had[rows], got[rows]], 0)
            down = jnp.concatenate([got[rows], had[rows]], 0)
            value = jnp.where(core == 0, up, down)
            vector[8 * y : 8 * y + 8, here] = value
            halo[8 * y : 8 * y + 8, here] = value * spread


def vectors(place, mine, other, base, aux):
    return pl.pallas_call(
        vectors_kernel,
        out_shape=(
            jax.ShapeDtypeStruct((40, WIDE), f32),
            jax.ShapeDtypeStruct((ROWS, CHIP), f32),
            jax.ShapeDtypeStruct((8, 128), f32),
        ),
        in_specs=smem(1) + vmem(4),
        out_specs=vmem(3),
        compiler_params=params(4),
        name="vectors",
    )(place, mine, other, base, aux)


def distance(left, right):
    return jnp.maximum(dot(left, right), 1e-30)


def covariance(x):
    z = jnp.maximum(STRETCH - pl.reciprocal(lax.rsqrt(x), approx=True), 0.0)
    z2 = z * z
    return z2 * z2 * (TOP - z)


def times(parts, tile):
    th, tl = two_parts(tile)
    pair = dot(jnp.concatenate(parts, 0), th)
    return (pair[0:ROWS] + pair[ROWS:]) + dot(parts[0], tl)


def sides(count, offset, place, own, halo, first, mask, left, top):
    column = 24 if offset == 0 else 8 * (offset - 1)
    flags = jnp.where(place[1] == 0, own[...], halo[32:40, CHIP:])
    for a in range(8):
        mask[:, a * BLOCK : (a + 1) * BLOCK] = jnp.broadcast_to(
            flags[:, column + a : column + a + 1], (8, BLOCK)
        )
    width = count * BLOCK
    sub = lax.broadcasted_iota(jnp.int32, (8, width), 0)
    points = halo[32:40, 0:width]
    b1, b2, b3 = three_parts(
        jnp.where(sub < 3, points, jnp.where(sub < 5, 1.0, 0.0))
    )
    left[0:width, :] = jnp.concatenate([b1, b2, b1, b2, b3, b1], 0).T.astype(bf16)
    sub = lax.broadcasted_iota(jnp.int32, (8, CHIP), 0)
    a1 = first[...]
    for b in range(count):
        row = jnp.broadcast_to(mask[b : b + 1, :], (8, CHIP))
        top[16 * b : 16 * b + 16, :] = jnp.concatenate(
            [jnp.where(sub == 4, row, a1), a1], 0
        ).astype(bf16)


def side_scratch(count):
    return [
        pltpu.VMEM((8, CHIP), f32),
        pltpu.VMEM((count * BLOCK, 48), bf16),
        pltpu.VMEM((count * 16, CHIP), bf16),
        pltpu.VMEM((2, BLOCK, BLOCK), f32),
    ]


def make_tiles(jobs, left, top, right, kept, held, total):
    def start(n):
        block, here, _, _, _ = jobs[n]
        rows = pl.ds(pl.multiple_of(block * BLOCK, BLOCK), BLOCK)
        upper = pl.ds(pl.multiple_of(block * 16, 16), 16)
        side = jnp.concatenate([top[upper, here], right[:, here]], 0)
        held[n % 2] = distance(left[rows, :], side)

    start(0)
    for n, (_, here, rows, columns, parts) in enumerate(jobs):
        if n + 1 < len(jobs):
            start(n + 1)
        kept[rows, columns] = covariance(held[n % 2])
        total[:, here] += times(parts, kept[rows, columns])


def tiles0_kernel(
    place, own, halo, first, right, kept, total, mask, left, top, held
):
    sides(4, 0, place, own, halo, first, mask, left, top)
    total[...] = jnp.zeros_like(total)
    jobs = []
    for b in range(4):
        rows = slice(b * BLOCK, (b + 1) * BLOCK)
        parts = two_parts(halo[0:ROWS, rows])
        for a in range(8):
            here = slice(a * BLOCK, (a + 1) * BLOCK)
            jobs.append((b, here, rows, here, parts))
    make_tiles(jobs, left, top, right, kept, held, total)


def tiles0(place, own, halo, first, right):
    return pl.pallas_call(
        tiles0_kernel,
        out_shape=(
            pltpu.VMEM((HALF, CHIP), f32),
            jax.ShapeDtypeStruct((ROWS, CHIP), f32),
        ),
        in_specs=smem(1) + vmem(4),
        out_specs=vmem(2),
        scratch_shapes=side_scratch(4),
        compiler_params=params(3),
        name="tiles0",
    )(place, own, halo, first, right)


def tiles_kernel(
    offset,
    place,
    own,
    halo,
    first,
    right,
    before,
    kept,
    total,
    mask,
    left,
    top,
    held,
):
    sides(8, offset, place, own, halo, first, mask, left, top)
    total[...] = before[...]

    def four_blocks(i, carry):
        jobs = []
        for n in range(4):
            b = 4 * i + n
            rows = pl.ds(pl.multiple_of(b * BLOCK, BLOCK), BLOCK)
            parts = two_parts(halo[0:ROWS, rows])
            for a in range(8):
                here = slice(a * BLOCK, (a + 1) * BLOCK)
                jobs.append((b, here, rows, here, parts))
        make_tiles(jobs, left, top, right, kept, held, total)
        return carry

    lax.fori_loop(0, 2, four_blocks, 0)


def tiles(offset, place, own, halo, first, right, before):
    return pl.pallas_call(
        functools.partial(tiles_kernel, offset),
        out_shape=(
            pltpu.VMEM((CHIP, CHIP), f32),
            jax.ShapeDtypeStruct((ROWS, CHIP), f32),
        ),
        in_specs=smem(1) + vmem(5),
        out_specs=vmem(2),
        scratch_shapes=side_scratch(8),
        compiler_params=params(4),
        name=f"tiles{offset}",
    )(place, own, halo, first, right, before)


def edge_kernel(
    place, own, halo, first, right, before, kept, total, mask, left, top, held
):
    sides(7, 3, place, own, halo, first, mask, left, top)
    total[...] = before[...]
    jobs = []
    for j in range(7):
        rows = slice(j * BLOCK, (j + 1) * BLOCK)
        parts = two_parts(halo[0:ROWS, rows])
        for a in range(j + 1, 8):
            here = slice(a * BLOCK, (a + 1) * BLOCK)
            at = (a * (a - 1) // 2 + j) * BLOCK
            jobs.append((j, here, slice(at, at + BLOCK), slice(0, BLOCK), parts))
    make_tiles(jobs, left, top, right, kept, held, total)


def edge_tiles(place, own, halo, first, right, before):
    return pl.pallas_call(
        edge_kernel,
        out_shape=(
            pltpu.VMEM((28 * BLOCK, BLOCK), f32),
            jax.ShapeDtypeStruct((ROWS, CHIP), f32),
        ),
        in_specs=smem(1) + vmem(5),
        out_specs=vmem(2),
        scratch_shapes=side_scratch(7),
        compiler_params=params(4),
        name="tiles3",
    )(place, own, halo, first, right, before)


def apply_kernel(depth, vector, kept, before, total):
    uh, ul = two_parts(vector[0:ROWS, 0:depth])

    def half(i, carry):
        for n in range(0, HALF, BLOCK):
            here = pl.ds(pl.multiple_of(i * HALF + n, BLOCK), BLOCK)
            value = before[:, here]
            for k in range(0, depth, BLOCK):
                rows = slice(k, k + BLOCK)
                value = value + times((uh[:, rows], ul[:, rows]), kept[rows, here])
            total[:, here] = value
        return carry

    lax.fori_loop(0, CHIP // HALF, half, 0)


def apply(vector, kept, before):
    return pl.pallas_call(
        functools.partial(apply_kernel, kept.shape[0]),
        out_shape=jax.ShapeDtypeStruct((ROWS, CHIP), f32),
        in_specs=vmem(3),
        out_specs=vmem(1)[0],
        compiler_params=params(3),
        name="apply",
    )(vector, kept, before)


def edge_apply_kernel(vector, kept, before, total):
    uh, ul = two_parts(vector[0:ROWS, 0 : 7 * BLOCK])
    total[:, 0:BLOCK] = before[:, 0:BLOCK]
    for a in range(1, 8):
        here = slice(a * BLOCK, (a + 1) * BLOCK)
        value = before[:, here]
        for j in range(a):
            rows = slice(j * BLOCK, (j + 1) * BLOCK)
            at = (a * (a - 1) // 2 + j) * BLOCK
            parts = (uh[:, rows], ul[:, rows])
            value = value + times(parts, kept[at : at + BLOCK, :])
        total[:, here] = value


def edge_apply(vector, kept, before):
    return pl.pallas_call(
        edge_apply_kernel,
        out_shape=jax.ShapeDtypeStruct((ROWS, CHIP), f32),
        in_specs=vmem(3),
        out_specs=vmem(1)[0],
        compiler_params=params(3),
        name="apply3",
    )(vector, kept, before)


def combine_kernel(mine, other, aux, vector, image, scaled):
    for j in range(8):
        here = slice(j * BLOCK, (j + 1) * BLOCK)
        there = slice((7 - j) * BLOCK, (8 - j) * BLOCK)
        spread = aux[0:1, here]
        value = (mine[:, here] + other[:, there]) * spread
        value = value + aux[1:2, here] * vector[:, here]
        image[:, here] = value
        scaled[:, here] = value * spread


def combine(mine, other, aux, vector):
    shape = jax.ShapeDtypeStruct((ROWS, CHIP), f32)
    return pl.pallas_call(
        combine_kernel,
        out_shape=(shape, shape),
        in_specs=vmem(4),
        out_specs=vmem(2),
        compiler_params=params(3),
        name="combine",
    )(mine, other, aux, vector)


def finish_kernel(
    place, mine, other, aux, vector, image, own, ahead1, ahead2, ahead3, last, packed
):
    row_at, core = place[2], place[1]
    sums = [jnp.zeros((ROWS, 1), f32) for _ in range(4)]
    for j in range(8):
        here = slice(j * BLOCK, (j + 1) * BLOCK)
        there = slice((7 - j) * BLOCK, (8 - j) * BLOCK)
        start, first = vector[:, here], image[:, here]
        value = (mine[:, here] + other[:, there]) * aux[0:1, here]
        value = value + aux[1:2, here] * first
        last[:, here] = value
        terms = (start * start, start * first, first * first, first * value)
        sums = [s + jnp.sum(t, axis=1, keepdims=True) for s, t in zip(sums, terms)]
    lane = lax.broadcasted_iota(jnp.int32, (ROWS, 128), 1)
    row = jnp.zeros((ROWS, 128), f32)
    for i in range(4):
        row = jnp.where(lane == i, sums[i], row)
    packed[...] = row
    for step, out in enumerate((own, ahead1, ahead2, ahead3)):
        rows = pl.ds(pl.multiple_of(lax.rem(row_at + step, 4) * 8, 8), 8)

        def chosen(value):
            return jnp.where(core == 0, value[0:4], value[4:8])

        for j in range(8):
            here = slice(j * BLOCK, (j + 1) * BLOCK)
            to = (j + core * (7 - 2 * j)) * BLOCK
            out[:, pl.ds(pl.multiple_of(to, BLOCK), BLOCK)] = chosen(image[rows, here])
            out[:, pl.ds(pl.multiple_of(CHIP + to, BLOCK), BLOCK)] = chosen(
                last[rows, here]
            )
        out[:, 2 * CHIP :] = chosen(packed[rows, :])


def finish(place, mine, other, aux, vector, image):
    part = jax.ShapeDtypeStruct((4, 2 * CHIP + 128), f32)
    return pl.pallas_call(
        finish_kernel,
        out_shape=(part, part, part, part),
        in_specs=smem(1) + vmem(5),
        out_specs=vmem(4),
        scratch_shapes=[pltpu.VMEM((ROWS, CHIP), f32), pltpu.VMEM((ROWS, 128), f32)],
        compiler_params=params(4),
        name="finish",
    )(place, mine, other, aux, vector, image)


def region_sums_kernel(own, behind1, behind2, behind3, out):
    total = own[:, 2 * CHIP :] + behind1[:, 2 * CHIP :]
    total = total + (behind2[:, 2 * CHIP :] + behind3[:, 2 * CHIP :])
    out[...] = jnp.broadcast_to(total[None], out.shape)


def region_sums(regions, parts):
    return pl.pallas_call(
        region_sums_kernel,
        out_shape=jax.ShapeDtypeStruct((regions, 4, 128), f32),
        in_specs=vmem(4),
        out_specs=vmem(1)[0],
        compiler_params=params(4),
        name="region_sums",
    )(*parts)


def result_kernel(
    place, sums, innovations, own, behind1, behind2, behind3, field, residual
):
    totals = jnp.sum(sums[...], axis=0)
    bb, bk, kk, kl = (totals[:, i : i + 1] for i in range(4))
    alpha = bb / bk
    norm = alpha * alpha * kk - 2.0 * alpha * bk + bb
    grown = 1.0 + norm / bb
    energy = grown * grown * bk - 2.0 * alpha * grown * kk + alpha * alpha * kl
    step = norm / energy
    for back, part in enumerate((own, behind1, behind2, behind3)):
        at = chip_at(place, (place[2] - back) & 3) * CHIP
        here = pl.ds(pl.multiple_of(at, CHIP), CHIP)
        start = innovations[:, here]
        first, last = part[:, 0:CHIP], part[:, CHIP : 2 * CHIP]
        field[:, here] = alpha * start + step * (grown * start - alpha * first)
        residual[:, here] = (
            start - alpha * first - step * (grown * first - alpha * last)
        )


def result(place, sums, innovations, parts):
    shape = jax.ShapeDtypeStruct(innovations.shape, f32)
    return pl.pallas_call(
        result_kernel,
        out_shape=(shape, shape),
        in_specs=smem(1) + vmem(6),
        out_specs=vmem(2),
        compiler_params=params(4),
        name="result",
    )(place, sums, innovations, *parts)


def device(chip, core):
    region, place = divmod(chip, 4)
    return 8 * region + 2 * (place ^ (place >> 1) ^ (2 * (region % 2))) + core


def neighbours(block, step, chips):
    route = []
    for m in range(chips - step):
        route.append((device(m + step, 0), device(m, 0)))
        route.append((device(m, 1), device(m + step, 1)))
    return lax.ppermute(block, AXES, route)


def sibling(block, chips):
    route = [(i, i ^ 1) for i in range(2 * chips)]
    return lax.ppermute(block, AXES, route)


after = lax.optimization_barrier


def along_y(parts):
    columns = lax.axis_size("cols")
    return [
        lax.ppermute(
            part, "cols", [(i, (i + 2 * step) % columns) for i in range(columns)]
        )
        for step, part in enumerate(parts, 1)
    ]


def per_device(
    innovations, coords, background_std, obs_variance, block_count, pair_list, pair_count
):
    regions = lax.axis_size("region")
    chips = regions * lax.axis_size("cols") // 2
    column = lax.axis_index("cols")
    row_at = column // 2
    odd = lax.axis_index("region") % 2
    turned = row_at ^ (2 * odd)
    place = jnp.stack([turned ^ (turned >> 1), column % 2, row_at, odd])

    own, *ahead = split(place, pair_count, pair_list, innovations)
    behind = along_y(ahead)
    base, aux, first, right = points(
        place,
        block_count,
        coords,
        background_std.reshape(1, -1),
        obs_variance.reshape(1, -1),
    )
    behind, base, aux = after((behind, base, aux))
    half = assemble(place, own, *behind)
    halo, vector, flags = vectors(place, half, sibling(half, chips), base, aux)

    halos = [neighbours(halo, step, chips) for step in (1, 2, 3)]
    made, total = tiles0(place, flags, halo, first, right)
    kept = [made]
    for k in (1, 2):
        made, total = tiles(k, place, flags, halos[k - 1], first, right, total)
        kept.append(made)
    made, part = edge_tiles(place, flags, halos[2], first, right, total)
    kept.append(made)
    image, scaled = combine(part, sibling(part, chips), aux, vector)

    halos = [scaled] + [neighbours(scaled, step, chips) for step in (1, 2, 3)]
    total = jnp.zeros((ROWS, CHIP), f32)
    for k in range(3):
        total = apply(halos[k], kept[k], total)
    part = edge_apply(halos[3], kept[3], total)
    own, *ahead = finish(place, part, sibling(part, chips), aux, vector, image)

    parts = [own] + along_y(ahead)
    sums = lax.all_to_all(region_sums(regions, parts), "region", 0, 0, tiled=True)
    return result(place, sums, innovations, parts)


def solution(mesh):
    placed = (
        P("cols", "region"),
        P(None, "region"),
        P("region"),
        P("region"),
        P("region"),
        P(None, ("region", "cols")),
        P(("region", "cols")),
    )
    return jax.shard_map(
        per_device,
        mesh=mesh,
        in_specs=placed,
        out_specs=(P("cols", "region"), P("cols", "region")),
        check_vma=False,
    )
```

profile of v0, /device:TPU:2, one launch (start us, length us, event | category | flops | bytes accessed | tf_op | source)
XLA Modules:
  0.0 109.5 jit_solution(16060161263120298)
XLA Ops:
  1.3 0.1 pad_add_fusion.place
  1.4 1.4 %split.1 = (f32[4,2176]{1,0:T(4,128)S(1)}, f32[4,2176]{1,0:T(4,128)S(1)}, f32[4,2176]{1,0:T(4,128)S(1)}, f32[4,2176]{1,0:T(4,128)S(1)}) custom-call(s32[4]{0:T(128)S(1)} %pad_add_fusion.place, s32[1]{0:T(128)S(6)} %copy.9.count, s32[2,96]{1,0:T(2,128)} %pairs.1, f32[4,8192]{1,0:T(4,128)} %innovations.3), custom_call_target="tpu_custom_call" | custom-call | tf_op jit(solution)/shard_map/split/pallas_call | solution.py:96
  2.8 1.7 %collective-permute-start = (f32[4,2176]{1,0:T(4,128)S(1)}, f32[4,2176]{1,0:T(4,128)S(1)}, u32[]{:S(2)}, u32[]{:S(2)}) collective-permute-start(f32[4,2176]{1,0:T(4,128)S(1)} %get-tuple-element.33), channel_id=1, source_target_pairs={{0,2},{1,3},{2,4},{3,5},{4,6},{5,7},{6,0},{7,1},{8,10},{9,11},{10,... | collective-permute-start | bytes 104456 | tf_op jit(solution)/shard_map/ppermute | solution.py:631
  4.5 2.9 %collective-permute-start.1 = (f32[4,2176]{1,0:T(4,128)S(1)}, f32[4,2176]{1,0:T(4,128)S(1)}, u32[]{:S(2)}, u32[]{:S(2)}) collective-permute-start(f32[4,2176]{1,0:T(4,128)S(1)} %get-tuple-element.34), channel_id=1, source_target_pairs={{0,4},{1,5},{2,6},{3,7},{4,0},{5,1},{6,2},{7,3},{8,12},{9,13},{10,... | collective-permute-start | bytes 104456 | tf_op jit(solution)/shard_map/ppermute | solution.py:631
  7.4 1.3 %collective-permute-start.2 = (f32[4,2176]{1,0:T(4,128)S(1)}, f32[4,2176]{1,0:T(4,128)S(1)}, u32[]{:S(2)}, u32[]{:S(2)}) collective-permute-start(f32[4,2176]{1,0:T(4,128)S(1)} %get-tuple-element.35), channel_id=1, source_target_pairs={{0,6},{1,7},{2,0},{3,1},{4,2},{5,3},{6,4},{7,5},{8,14},{9,15},{10,... | collective-permute-start | bytes 104456 | tf_op jit(solution)/shard_map/ppermute | solution.py:631
  8.7 1.4 %points.1 = (f32[8,2048]{1,0:T(8,128)S(1)}, f32[8,2048]{1,0:T(8,128)S(1)}, f32[8,2048]{1,0:T(8,128)S(1)}, bf16[32,2048]{1,0:T(8,128)(2,1)S(1)}) custom-call(s32[4]{0:T(128)S(1)} %pad_add_fusion.place, s32[32]{0:T(128)} %all_counts.1, f32[3,8192]{1,0:T(4,128)} %all_coords.1, f32[1,8192]{1,0:T(1,128)} %bitcast.6, f32[1,8192]{1,0:T(1,128)} %bitcast.7), custom_call_target="tpu_custom_call" | custom-call | tf_op jit(solution)/shard_map/points/pallas_call | solution.py:202
  10.1 0.0 collective-permute-done.behind1
  10.1 0.0 collective-permute-done.1.behind2
  10.2 1.1 %collective-permute-done.2.behind3 = f32[4,2176]{1,0:T(4,128)S(1)} collective-permute-done((f32[4,2176]{1,0:T(4,128)S(1)}, f32[4,2176]{1,0:T(4,128)S(1)}, u32[]{:S(2)}, u32[]{:S(2)}) %collective-permute-start.2) | collective-permute-done | bytes 34848 | tf_op jit(solution)/shard_map/ppermute | solution.py:631
  11.3 0.6 assemble.1.mine
  11.9 0.1 collective-permute-start.3
  12.0 1.3 %collective-permute-done.3.other = f32[16,2176]{1,0:T(8,128)S(1)} collective-permute-done((f32[16,2176]{1,0:T(8,128)S(1)}, f32[16,2176]{1,0:T(8,128)S(1)}, u32[]{:S(2)}, u32[]{:S(2)}) %collective-permute-start.3) | collective-permute-done | bytes 139296 | tf_op jit(solution)/shard_map/ppermute | solution.py:622
  13.3 0.9 vectors.1
  14.3 2.1 %collective-permute-start.6 = (f32[40,2176]{1,0:T(8,128)S(1)}, f32[40,2176]{1,0:T(8,128)S(1)}, u32[]{:S(2)}, u32[]{:S(2)}) collective-permute-start(f32[40,2176]{1,0:T(8,128)S(1)} %get-tuple-element.44.halo), channel_id=1, source_target_pairs={{2,0},{1,3},{6,2},{3,7},{4,6},{7,5},{12,4},{5,13},{14,12},{13,15},... | collective-permute-start | bytes 1044488 | tf_op jit(solution)/shard_map/ppermute | solution.py:617
  16.4 4.3 %collective-permute-start.5 = (f32[40,2176]{1,0:T(8,128)S(1)}, f32[40,2176]{1,0:T(8,128)S(1)}, u32[]{:S(2)}, u32[]{:S(2)}) collective-permute-start(f32[40,2176]{1,0:T(8,128)S(1)} %get-tuple-element.44.halo), channel_id=1, source_target_pairs={{6,0},{1,7},{4,2},{3,5},{12,6},{7,13},{14,4},{5,15},{10,12},{13,11... | collective-permute-start | bytes 1044488 | tf_op jit(solution)/shard_map/ppermute | solution.py:617
  20.7 4.8 %collective-permute-start.4 = (f32[40,2176]{1,0:T(8,128)S(1)}, f32[40,2176]{1,0:T(8,128)S(1)}, u32[]{:S(2)}, u32[]{:S(2)}) collective-permute-start(f32[40,2176]{1,0:T(8,128)S(1)} %get-tuple-element.44.halo), channel_id=1, source_target_pairs={{4,0},{1,5},{12,2},{3,13},{14,6},{7,15},{10,4},{5,11},{8,12},{13,9... | collective-permute-start | bytes 1044488 | tf_op jit(solution)/shard_map/ppermute | solution.py:617
  25.5 4.7 %tiles0.1 = (f32[1024,2048]{1,0:T(8,128)S(1)}, f32[32,2048]{1,0:T(8,128)S(1)}) custom-call(s32[4]{0:T(128)S(1)} %pad_add_fusion.place, f32[8,128]{1,0:T(8,128)S(1)} %get-tuple-element.43.own, f32[40,2176]{1,0:T(8,128)S(1)} %get-tuple-element.44.halo, f32[8,2048]{1,0:T(8,128)S(1)} %get-tuple-element.45.first, bf16[32,2048]{1,0:T(8,128)(2,1)S(1)} %get-tuple-element.46.right), custom_call_target="tpu_custom_call" | custom-call | tf_op jit(solution)/shard_map/tiles0/pallas_call | solution.py:341
  30.1 0.0 collective-permute-done.6.halo
  30.1 8.7 %tiles1.1 = (f32[2048,2048]{1,0:T(8,128)S(1)}, f32[32,2048]{1,0:T(8,128)S(1)}) custom-call(s32[4]{0:T(128)S(1)} %pad_add_fusion.place, f32[8,128]{1,0:T(8,128)S(1)} %get-tuple-element.43.own, f32[40,2176]{1,0:T(8,128)S(1)} %collective-permute-done.6.halo, f32[8,2048]{1,0:T(8,128)S(1)} %get-tuple-element.45.first, ...), custom_call_target="tpu_custom_call" | custom-call | tf_op jit(solution)/shard_map/tiles1/pallas_call | solution.py:389
  38.8 0.0 collective-permute-done.5.halo
  38.8 8.5 %tiles2.1 = (f32[2048,2048]{1,0:T(8,128)S(1)}, f32[32,2048]{1,0:T(8,128)S(1)}) custom-call(s32[4]{0:T(128)S(1)} %pad_add_fusion.place, f32[8,128]{1,0:T(8,128)S(1)} %get-tuple-element.43.own, f32[40,2176]{1,0:T(8,128)S(1)} %collective-permute-done.5.halo, f32[8,2048]{1,0:T(8,128)S(1)} %get-tuple-element.45.first, ...), custom_call_target="tpu_custom_call" | custom-call | tf_op jit(solution)/shard_map/tiles2/pallas_call | solution.py:389
  47.3 0.0 collective-permute-done.4.halo
  47.3 4.3 %tiles3.1 = (f32[7168,256]{1,0:T(8,128)S(1)}, f32[32,2048]{1,0:T(8,128)S(1)}) custom-call(s32[4]{0:T(128)S(1)} %pad_add_fusion.place, f32[8,128]{1,0:T(8,128)S(1)} %get-tuple-element.43.own, f32[40,2176]{1,0:T(8,128)S(1)} %collective-permute-done.4.halo, f32[8,2048]{1,0:T(8,128)S(1)} %get-tuple-element.45.first, ...), custom_call_target="tpu_custom_call" | custom-call | tf_op jit(solution)/shard_map/tiles3/pallas_call | solution.py:420
  51.6 0.0 collective-permute-start.7
  51.6 1.5 %collective-permute-done.7.other = f32[32,2048]{1,0:T(8,128)S(1)} collective-permute-done((f32[32,2048]{1,0:T(8,128)S(1)}, f32[32,2048]{1,0:T(8,128)S(1)}, u32[]{:S(2)}, u32[]{:S(2)}) %collective-permute-start.7) | collective-permute-done | bytes 262176 | tf_op jit(solution)/shard_map/ppermute | solution.py:622
  53.1 0.1 combine.1
  53.2 3.3 %collective-permute-start.10 = (f32[32,2048]{1,0:T(8,128)S(1)}, f32[32,2048]{1,0:T(8,128)S(1)}, u32[]{:S(2)}, u32[]{:S(2)}) collective-permute-start(f32[32,2048]{1,0:T(8,128)S(1)} %get-tuple-element.52.vector), channel_id=1, source_target_pairs={{2,0},{1,3},{6,2},{3,7},{4,6},{7,5},{12,4},{5,13},{14,12},{13,15},... | collective-permute-start | bytes 786440 | tf_op jit(solution)/shard_map/ppermute | solution.py:617
  56.5 5.0 %collective-permute-start.9 = (f32[32,2048]{1,0:T(8,128)S(1)}, f32[32,2048]{1,0:T(8,128)S(1)}, u32[]{:S(2)}, u32[]{:S(2)}) collective-permute-start(f32[32,2048]{1,0:T(8,128)S(1)} %get-tuple-element.52.vector), channel_id=1, source_target_pairs={{6,0},{1,7},{4,2},{3,5},{12,6},{7,13},{14,4},{5,15},{10,12},{13,11... | collective-permute-start | bytes 786440 | tf_op jit(solution)/shard_map/ppermute | solution.py:617
  61.5 5.1 %collective-permute-start.8 = (f32[32,2048]{1,0:T(8,128)S(1)}, f32[32,2048]{1,0:T(8,128)S(1)}, u32[]{:S(2)}, u32[]{:S(2)}) collective-permute-start(f32[32,2048]{1,0:T(8,128)S(1)} %get-tuple-element.52.vector), channel_id=1, source_target_pairs={{4,0},{1,5},{12,2},{3,13},{14,6},{7,15},{10,4},{5,11},{8,12},{13,9... | collective-permute-start | bytes 786440 | tf_op jit(solution)/shard_map/ppermute | solution.py:617
  66.7 2.1 %apply.3.before = f32[32,2048]{1,0:T(8,128)S(1)} custom-call(f32[32,2048]{1,0:T(8,128)S(1)} %get-tuple-element.52.vector, f32[1024,2048]{1,0:T(8,128)S(1)} %get-tuple-element.56.kept, f32[32,2048]{1,0:T(8,128)S(1)} %broadcast_in_dim.3.before), custom_call_target="tpu_custom_call" | custom-call | tf_op jit(solution)/shard_map/apply/pallas_call | solution.py:451
  68.8 0.0 collective-permute-done.10.vector
  68.8 3.5 %apply.4.before = f32[32,2048]{1,0:T(8,128)S(1)} custom-call(f32[32,2048]{1,0:T(8,128)S(1)} %collective-permute-done.10.vector, f32[2048,2048]{1,0:T(8,128)S(1)} %get-tuple-element.55.kept, f32[32,2048]{1,0:T(8,128)S(1)} %apply.3.before), custom_call_target="tpu_custom_call" | custom-call | tf_op jit(solution)/shard_map/apply/pallas_call | solution.py:451
  72.2 0.0 copy-start
  72.3 0.0 collective-permute-done.9.vector
  72.3 3.5 %apply.5.before = f32[32,2048]{1,0:T(8,128)S(1)} custom-call(f32[32,2048]{1,0:T(8,128)S(1)} %collective-permute-done.9.vector, f32[2048,2048]{1,0:T(8,128)S(1)} %get-tuple-element.54.kept, f32[32,2048]{1,0:T(8,128)S(1)} %apply.4.before), custom_call_target="tpu_custom_call" | custom-call | tf_op jit(solution)/shard_map/apply/pallas_call | solution.py:451
  75.7 0.0 collective-permute-done.8.vector
  75.7 1.6 %apply3.1.mine = f32[32,2048]{1,0:T(8,128)S(1)} custom-call(f32[32,2048]{1,0:T(8,128)S(1)} %collective-permute-done.8.vector, f32[7168,256]{1,0:T(8,128)S(1)} %get-tuple-element.53.kept, f32[32,2048]{1,0:T(8,128)S(1)} %apply.5.before), custom_call_target="tpu_custom_call" | custom-call | tf_op jit(solution)/shard_map/apply3/pallas_call | solution.py:476
  77.3 0.0 collective-permute-start.11
  77.4 1.5 %collective-permute-done.11.other = f32[32,2048]{1,0:T(8,128)S(1)} collective-permute-done((f32[32,2048]{1,0:T(8,128)S(1)}, f32[32,2048]{1,0:T(8,128)S(1)}, u32[]{:S(2)}, u32[]{:S(2)}) %collective-permute-start.11) | collective-permute-done | bytes 262176 | tf_op jit(solution)/shard_map/ppermute | solution.py:622
  78.9 0.8 finish.1
  79.7 0.5 collective-permute-start.12
  80.2 2.6 %collective-permute-start.13 = (f32[4,4224]{1,0:T(4,128)S(1)}, f32[4,4224]{1,0:T(4,128)S(1)}, u32[]{:S(2)}, u32[]{:S(2)}) collective-permute-start(f32[4,4224]{1,0:T(4,128)S(1)} %get-tuple-element.60), channel_id=1, source_target_pairs={{0,4},{1,5},{2,6},{3,7},{4,0},{5,1},{6,2},{7,3},{8,12},{9,13},{10,... | collective-permute-start | bytes 202760 | tf_op jit(solution)/shard_map/ppermute | solution.py:631
  82.8 1.3 %collective-permute-start.14 = (f32[4,4224]{1,0:T(4,128)S(1)}, f32[4,4224]{1,0:T(4,128)S(1)}, u32[]{:S(2)}, u32[]{:S(2)}) collective-permute-start(f32[4,4224]{1,0:T(4,128)S(1)} %get-tuple-element.61), channel_id=1, source_target_pairs={{0,6},{1,7},{2,0},{3,1},{4,2},{5,3},{6,4},{7,5},{8,14},{9,15},{10,... | collective-permute-start | bytes 202760 | tf_op jit(solution)/shard_map/ppermute | solution.py:631
  84.1 1.8 %collective-permute-done.12.behind1 = f32[4,4224]{1,0:T(4,128)S(1)} collective-permute-done((f32[4,4224]{1,0:T(4,128)S(1)}, f32[4,4224]{1,0:T(4,128)S(1)}, u32[]{:S(2)}, u32[]{:S(2)}) %collective-permute-start.12) | collective-permute-done | bytes 67616 | tf_op jit(solution)/shard_map/ppermute | solution.py:631
  85.9 0.7 collective-permute-done.13.behind2
  86.6 0.6 collective-permute-done.14.behind3
  87.2 20.8 %all_to_all.5.sums = f32[32,4,128]{2,1,0:T(4,128)S(1)} all-to-all(f32[32,4,128]{2,1,0:T(4,128)S(1)} %region_sums.1), channel_id=1, replica_groups=mesh['region'=32,'cols'=8] {'region'}, dimensions={0} | all-to-all | bytes 131072 | tf_op jit(solution)/shard_map/all_to_all | solution.py:680
  108.0 0.0 copy-done
  108.0 1.5 %result.1 = (f32[4,8192]{1,0:T(4,128)}, f32[4,8192]{1,0:T(4,128)}) custom-call(s32[4]{0:T(128)S(1)} %pad_add_fusion.place, f32[32,4,128]{2,1,0:T(4,128)S(1)} %all_to_all.5.sums, f32[4,8192]{1,0:T(4,128)S(1)} %copy-done, f32[4,4224]{1,0:T(4,128)S(1)} %get-tuple-element.58.own, f32[4,4224]{1,0:T(4,128)S(1)} %collective-permute-done.12.behind1, ...), custom_call_target="tpu_custom_call" | custom-call | tf_op jit(solution)/shard_map/result/pallas_call | solution.py:597
  (2 shorter events, 0.0 us)
Async XLA Ops:
  2.8 7.3 %collective-permute-start = (f32[4,2176]{1,0:T(4,128)S(1)}, f32[4,2176]{1,0:T(4,128)S(1)}, u32[]{:S(2)}, u32[]{:S(2)}) collective-permute-start(f32[4,2176]{1,0:T(4,128)S(1)} %get-tuple-element.33), channel_id=1, source_target_pairs={{0,2},{1,3},{2,4},{3,5},{4,6},{5,7},{6,0},{7,1},{8,10},{9,11},{10,... | collective-permute-start | bytes 104456 | tf_op jit(solution)/shard_map/ppermute | solution.py:631
  4.5 5.7 %collective-permute-start.1 = (f32[4,2176]{1,0:T(4,128)S(1)}, f32[4,2176]{1,0:T(4,128)S(1)}, u32[]{:S(2)}, u32[]{:S(2)}) collective-permute-start(f32[4,2176]{1,0:T(4,128)S(1)} %get-tuple-element.34), channel_id=1, source_target_pairs={{0,4},{1,5},{2,6},{3,7},{4,0},{5,1},{6,2},{7,3},{8,12},{9,13},{10,... | collective-permute-start | bytes 104456 | tf_op jit(solution)/shard_map/ppermute | solution.py:631
  7.4 3.9 %collective-permute-start.2 = (f32[4,2176]{1,0:T(4,128)S(1)}, f32[4,2176]{1,0:T(4,128)S(1)}, u32[]{:S(2)}, u32[]{:S(2)}) collective-permute-start(f32[4,2176]{1,0:T(4,128)S(1)} %get-tuple-element.35), channel_id=1, source_target_pairs={{0,6},{1,7},{2,0},{3,1},{4,2},{5,3},{6,4},{7,5},{8,14},{9,15},{10,... | collective-permute-start | bytes 104456 | tf_op jit(solution)/shard_map/ppermute | solution.py:631
  11.9 1.4 %collective-permute-start.3 = (f32[16,2176]{1,0:T(8,128)S(1)}, f32[16,2176]{1,0:T(8,128)S(1)}, u32[]{:S(2)}, u32[]{:S(2)}) collective-permute-start(f32[16,2176]{1,0:T(8,128)S(1)} %assemble.1.mine), channel_id=1, source_target_pairs={{0,1},{1,0},{2,3},{3,2},{4,5},{5,4},{6,7},{7,6},{8,9},{9,8},{10,11... | collective-permute-start | bytes 417800 | tf_op jit(solution)/shard_map/ppermute | solution.py:622
  14.3 15.9 %collective-permute-start.6 = (f32[40,2176]{1,0:T(8,128)S(1)}, f32[40,2176]{1,0:T(8,128)S(1)}, u32[]{:S(2)}, u32[]{:S(2)}) collective-permute-start(f32[40,2176]{1,0:T(8,128)S(1)} %get-tuple-element.44.halo), channel_id=1, source_target_pairs={{2,0},{1,3},{6,2},{3,7},{4,6},{7,5},{12,4},{5,13},{14,12},{13,15},... | collective-permute-start | bytes 1044488 | tf_op jit(solution)/shard_map/ppermute | solution.py:617
  16.4 22.4 %collective-permute-start.5 = (f32[40,2176]{1,0:T(8,128)S(1)}, f32[40,2176]{1,0:T(8,128)S(1)}, u32[]{:S(2)}, u32[]{:S(2)}) collective-permute-start(f32[40,2176]{1,0:T(8,128)S(1)} %get-tuple-element.44.halo), channel_id=1, source_target_pairs={{6,0},{1,7},{4,2},{3,5},{12,6},{7,13},{14,4},{5,15},{10,12},{13,11... | collective-permute-start | bytes 1044488 | tf_op jit(solution)/shard_map/ppermute | solution.py:617
  20.7 26.6 %collective-permute-start.4 = (f32[40,2176]{1,0:T(8,128)S(1)}, f32[40,2176]{1,0:T(8,128)S(1)}, u32[]{:S(2)}, u32[]{:S(2)}) collective-permute-start(f32[40,2176]{1,0:T(8,128)S(1)} %get-tuple-element.44.halo), channel_id=1, source_target_pairs={{4,0},{1,5},{12,2},{3,13},{14,6},{7,15},{10,4},{5,11},{8,12},{13,9... | collective-permute-start | bytes 1044488 | tf_op jit(solution)/shard_map/ppermute | solution.py:617
  51.6 1.6 %collective-permute-start.7 = (f32[32,2048]{1,0:T(8,128)S(1)}, f32[32,2048]{1,0:T(8,128)S(1)}, u32[]{:S(2)}, u32[]{:S(2)}) collective-permute-start(f32[32,2048]{1,0:T(8,128)S(1)} %get-tuple-element.50.mine), channel_id=1, source_target_pairs={{0,1},{1,0},{2,3},{3,2},{4,5},{5,4},{6,7},{7,6},{8,9},{9,8},{10,11... | collective-permute-start | bytes 786440 | tf_op jit(solution)/shard_map/ppermute | solution.py:622
  53.2 15.6 %collective-permute-start.10 = (f32[32,2048]{1,0:T(8,128)S(1)}, f32[32,2048]{1,0:T(8,128)S(1)}, u32[]{:S(2)}, u32[]{:S(2)}) collective-permute-start(f32[32,2048]{1,0:T(8,128)S(1)} %get-tuple-element.52.vector), channel_id=1, source_target_pairs={{2,0},{1,3},{6,2},{3,7},{4,6},{7,5},{12,4},{5,13},{14,12},{13,15},... | collective-permute-start | bytes 786440 | tf_op jit(solution)/shard_map/ppermute | solution.py:617
  56.5 15.7 %collective-permute-start.9 = (f32[32,2048]{1,0:T(8,128)S(1)}, f32[32,2048]{1,0:T(8,128)S(1)}, u32[]{:S(2)}, u32[]{:S(2)}) collective-permute-start(f32[32,2048]{1,0:T(8,128)S(1)} %get-tuple-element.52.vector), channel_id=1, source_target_pairs={{6,0},{1,7},{4,2},{3,5},{12,6},{7,13},{14,4},{5,15},{10,12},{13,11... | collective-permute-start | bytes 786440 | tf_op jit(solution)/shard_map/ppermute | solution.py:617
  61.5 14.2 %collective-permute-start.8 = (f32[32,2048]{1,0:T(8,128)S(1)}, f32[32,2048]{1,0:T(8,128)S(1)}, u32[]{:S(2)}, u32[]{:S(2)}) collective-permute-start(f32[32,2048]{1,0:T(8,128)S(1)} %get-tuple-element.52.vector), channel_id=1, source_target_pairs={{4,0},{1,5},{12,2},{3,13},{14,6},{7,15},{10,4},{5,11},{8,12},{13,9... | collective-permute-start | bytes 786440 | tf_op jit(solution)/shard_map/ppermute | solution.py:617
  72.2 35.7 %copy-start = (f32[4,8192]{1,0:T(4,128)S(1)}, f32[4,8192]{1,0:T(4,128)}, u32[]{:S(2)}) copy-start(f32[4,8192]{1,0:T(4,128)} %innovations.3) | copy-start | bytes 393220
  77.3 1.6 %collective-permute-start.11 = (f32[32,2048]{1,0:T(8,128)S(1)}, f32[32,2048]{1,0:T(8,128)S(1)}, u32[]{:S(2)}, u32[]{:S(2)}) collective-permute-start(f32[32,2048]{1,0:T(8,128)S(1)} %apply3.1.mine), channel_id=1, source_target_pairs={{0,1},{1,0},{2,3},{3,2},{4,5},{5,4},{6,7},{7,6},{8,9},{9,8},{10,11... | collective-permute-start | bytes 786440 | tf_op jit(solution)/shard_map/ppermute | solution.py:622
  79.7 6.2 %collective-permute-start.12 = (f32[4,4224]{1,0:T(4,128)S(1)}, f32[4,4224]{1,0:T(4,128)S(1)}, u32[]{:S(2)}, u32[]{:S(2)}) collective-permute-start(f32[4,4224]{1,0:T(4,128)S(1)} %get-tuple-element.59), channel_id=1, source_target_pairs={{0,2},{1,3},{2,4},{3,5},{4,6},{5,7},{6,0},{7,1},{8,10},{9,11},{10,... | collective-permute-start | bytes 202760 | tf_op jit(solution)/shard_map/ppermute | solution.py:631
  80.2 6.4 %collective-permute-start.13 = (f32[4,4224]{1,0:T(4,128)S(1)}, f32[4,4224]{1,0:T(4,128)S(1)}, u32[]{:S(2)}, u32[]{:S(2)}) collective-permute-start(f32[4,4224]{1,0:T(4,128)S(1)} %get-tuple-element.60), channel_id=1, source_target_pairs={{0,4},{1,5},{2,6},{3,7},{4,0},{5,1},{6,2},{7,3},{8,12},{9,13},{10,... | collective-permute-start | bytes 202760 | tf_op jit(solution)/shard_map/ppermute | solution.py:631
  82.8 4.4 %collective-permute-start.14 = (f32[4,4224]{1,0:T(4,128)S(1)}, f32[4,4224]{1,0:T(4,128)S(1)}, u32[]{:S(2)}, u32[]{:S(2)}) collective-permute-start(f32[4,4224]{1,0:T(4,128)S(1)} %get-tuple-element.61), channel_id=1, source_target_pairs={{0,6},{1,7},{2,0},{3,1},{4,2},{5,3},{6,4},{7,5},{8,14},{9,15},{10,... | collective-permute-start | bytes 202760 | tf_op jit(solution)/shard_map/ppermute | solution.py:631
where the time goes:
time: 110 us; the launch traced here: 109 us
  Pallas kernels  43.4 us (39%)
  starting transfers between devices  35.1 us (32%)
  blocking collectives  20.8 us (19%)
  waiting for transfers between devices  8.66 us (8%)
  between operations  1.5 us (1%)
    ppermute x6, starting transfers between devices, neighbours(): return lax.ppermute(block, AXES, route)  24.6 us
    all_to_all x1, blocking collectives, per_device(): lax.all_to_all(region_sums(regions, parts), 'region', 0, 0, tiled=True)  20.8 us
    pallas_call x2, Pallas kernels, tiles(): pl.pallas_call(functools.partial(tiles_kernel, offset), out_shape=(pltpu....  17.1 us
    ppermute x6, starting transfers between devices, along_y(): lax.ppermute(part, 'cols', [(i, (i + 2 * step) % columns) for i in range(...  10.3 us
    pallas_call x3, Pallas kernels, apply(): pl.pallas_call(functools.partial(apply_kernel, kept.shape[0]), out_shape=...  9 us
    pallas_call x1, Pallas kernels, tiles0(): pl.pallas_call(tiles0_kernel, out_shape=(pltpu.VMEM((HALF, CHIP), f32), j...  4.65 us
    ppermute x3, waiting for transfers between devices, sibling(): return lax.ppermute(block, AXES, route)  4.39 us
    pallas_call x1, Pallas kernels, edge_tiles(): pl.pallas_call(edge_kernel, out_shape=(pltpu.VMEM((28 * BLOCK, BLOCK), f3...  4.27 us
  transfers between devices with their start and end apart: 15, of which 7 were waited for; matrix products, arithmetic and copies ran while one was open for 0% of the time, Pallas kernels for 29%

commit v1 on v0

--- a/solution.py
+++ b/solution.py
@@ -433,18 +433,13 @@
 
 def apply_kernel(depth, vector, kept, before, total):
     uh, ul = two_parts(vector[0:ROWS, 0:depth])
-
-    def half(i, carry):
-        for n in range(0, HALF, BLOCK):
-            here = pl.ds(pl.multiple_of(i * HALF + n, BLOCK), BLOCK)
-            value = before[:, here]
-            for k in range(0, depth, BLOCK):
-                rows = slice(k, k + BLOCK)
-                value = value + times((uh[:, rows], ul[:, rows]), kept[rows, here])
-            total[:, here] = value
-        return carry
-
-    lax.fori_loop(0, CHIP // HALF, half, 0)
+    for n in range(0, CHIP, BLOCK):
+        here = slice(n, n + BLOCK)
+        value = before[:, here]
+        for k in range(0, depth, BLOCK):
+            rows = slice(k, k + BLOCK)
+            value = value + times((uh[:, rows], ul[:, rows]), kept[rows, here])
+        total[:, here] = value
 
 
 def apply(vector, kept, before):

time: 110 us -> 109 us (level)
  no operation moved by 1% of the time
where the time goes in v1:
time: 109 us
  Pallas kernels  42.6 us (39%)
  starting transfers between devices  35.5 us (33%)
  blocking collectives  20.7 us (19%)
  waiting for transfers between devices  8.7 us (8%)
  between operations  1.49 us (1%)
    ppermute x6, starting transfers between devices, neighbours(): return lax.ppermute(block, AXES, route)  24.8 us
    all_to_all x1, blocking collectives, per_device(): lax.all_to_all(region_sums(regions, parts), 'region', 0, 0, tiled=True)  20.7 us
    pallas_call x2, Pallas kernels, tiles(): pl.pallas_call(functools.partial(tiles_kernel, offset), out_shape=(pltpu....  17.1 us
    ppermute x6, starting transfers between devices, along_y(): lax.ppermute(part, 'cols', [(i, (i + 2 * step) % columns) for i in range(...  10.4 us
    pallas_call x3, Pallas kernels, apply(): pl.pallas_call(functools.partial(apply_kernel, kept.shape[0]), out_shape=...  8.23 us
    pallas_call x1, Pallas kernels, tiles0(): pl.pallas_call(tiles0_kernel, out_shape=(pltpu.VMEM((HALF, CHIP), f32), j...  4.65 us
    ppermute x3, waiting for transfers between devices, sibling(): return lax.ppermute(block, AXES, route)  4.39 us
    pallas_call x1, Pallas kernels, edge_tiles(): pl.pallas_call(edge_kernel, out_shape=(pltpu.VMEM((28 * BLOCK, BLOCK), f3...  4.27 us
  transfers between devices with their start and end apart: 15, of which 7 were waited for; matrix products, arithmetic and copies ran while one was open for 0% of the time, Pallas kernels for 29%

profile of v1, /device:TPU:2, one launch (start us, length us, event | category | flops | bytes accessed | tf_op | source)
XLA Modules:
  0.0 109.1 jit_solution(4487940045475946886)
XLA Ops:
  1.3 0.1 pad_add_fusion.place
  1.4 1.4 %split.1 = (f32[4,2176]{1,0:T(4,128)S(1)}, f32[4,2176]{1,0:T(4,128)S(1)}, f32[4,2176]{1,0:T(4,128)S(1)}, f32[4,2176]{1,0:T(4,128)S(1)}) custom-call(s32[4]{0:T(128)S(1)} %pad_add_fusion.place, s32[1]{0:T(128)S(6)} %copy.9.count, s32[2,96]{1,0:T(2,128)} %pairs.1, f32[4,8192]{1,0:T(4,128)} %innovations.3), custom_call_target="tpu_custom_call" | custom-call | tf_op jit(solution)/shard_map/split/pallas_call | solution.py:96
  2.8 1.7 %collective-permute-start = (f32[4,2176]{1,0:T(4,128)S(1)}, f32[4,2176]{1,0:T(4,128)S(1)}, u32[]{:S(2)}, u32[]{:S(2)}) collective-permute-start(f32[4,2176]{1,0:T(4,128)S(1)} %get-tuple-element.33), channel_id=1, source_target_pairs={{0,2},{1,3},{2,4},{3,5},{4,6},{5,7},{6,0},{7,1},{8,10},{9,11},{10,... | collective-permute-start | bytes 104456 | tf_op jit(solution)/shard_map/ppermute | solution.py:626
  4.5 2.9 %collective-permute-start.1 = (f32[4,2176]{1,0:T(4,128)S(1)}, f32[4,2176]{1,0:T(4,128)S(1)}, u32[]{:S(2)}, u32[]{:S(2)}) collective-permute-start(f32[4,2176]{1,0:T(4,128)S(1)} %get-tuple-element.34), channel_id=1, source_target_pairs={{0,4},{1,5},{2,6},{3,7},{4,0},{5,1},{6,2},{7,3},{8,12},{9,13},{10,... | collective-permute-start | bytes 104456 | tf_op jit(solution)/shard_map/ppermute | solution.py:626
  7.4 1.3 %collective-permute-start.2 = (f32[4,2176]{1,0:T(4,128)S(1)}, f32[4,2176]{1,0:T(4,128)S(1)}, u32[]{:S(2)}, u32[]{:S(2)}) collective-permute-start(f32[4,2176]{1,0:T(4,128)S(1)} %get-tuple-element.35), channel_id=1, source_target_pairs={{0,6},{1,7},{2,0},{3,1},{4,2},{5,3},{6,4},{7,5},{8,14},{9,15},{10,... | collective-permute-start | bytes 104456 | tf_op jit(solution)/shard_map/ppermute | solution.py:626
  8.7 1.4 %points.1 = (f32[8,2048]{1,0:T(8,128)S(1)}, f32[8,2048]{1,0:T(8,128)S(1)}, f32[8,2048]{1,0:T(8,128)S(1)}, bf16[32,2048]{1,0:T(8,128)(2,1)S(1)}) custom-call(s32[4]{0:T(128)S(1)} %pad_add_fusion.place, s32[32]{0:T(128)} %all_counts.1, f32[3,8192]{1,0:T(4,128)} %all_coords.1, f32[1,8192]{1,0:T(1,128)} %bitcast.6, f32[1,8192]{1,0:T(1,128)} %bitcast.7), custom_call_target="tpu_custom_call" | custom-call | tf_op jit(solution)/shard_map/points/pallas_call | solution.py:202
  10.1 0.0 collective-permute-done.behind1
  10.1 0.0 collective-permute-done.1.behind2
  10.2 1.1 %collective-permute-done.2.behind3 = f32[4,2176]{1,0:T(4,128)S(1)} collective-permute-done((f32[4,2176]{1,0:T(4,128)S(1)}, f32[4,2176]{1,0:T(4,128)S(1)}, u32[]{:S(2)}, u32[]{:S(2)}) %collective-permute-start.2) | collective-permute-done | bytes 34848 | tf_op jit(solution)/shard_map/ppermute | solution.py:626
  11.3 0.6 assemble.1.mine
  11.9 0.1 collective-permute-start.3
  12.0 1.3 %collective-permute-done.3.other = f32[16,2176]{1,0:T(8,128)S(1)} collective-permute-done((f32[16,2176]{1,0:T(8,128)S(1)}, f32[16,2176]{1,0:T(8,128)S(1)}, u32[]{:S(2)}, u32[]{:S(2)}) %collective-permute-start.3) | collective-permute-done | bytes 139296 | tf_op jit(solution)/shard_map/ppermute | solution.py:617
  13.3 0.9 vectors.1
  14.3 2.1 %collective-permute-start.6 = (f32[40,2176]{1,0:T(8,128)S(1)}, f32[40,2176]{1,0:T(8,128)S(1)}, u32[]{:S(2)}, u32[]{:S(2)}) collective-permute-start(f32[40,2176]{1,0:T(8,128)S(1)} %get-tuple-element.44.halo), channel_id=1, source_target_pairs={{2,0},{1,3},{6,2},{3,7},{4,6},{7,5},{12,4},{5,13},{14,12},{13,15},... | collective-permute-start | bytes 1044488 | tf_op jit(solution)/shard_map/ppermute | solution.py:612
  16.4 4.3 %collective-permute-start.5 = (f32[40,2176]{1,0:T(8,128)S(1)}, f32[40,2176]{1,0:T(8,128)S(1)}, u32[]{:S(2)}, u32[]{:S(2)}) collective-permute-start(f32[40,2176]{1,0:T(8,128)S(1)} %get-tuple-element.44.halo), channel_id=1, source_target_pairs={{6,0},{1,7},{4,2},{3,5},{12,6},{7,13},{14,4},{5,15},{10,12},{13,11... | collective-permute-start | bytes 1044488 | tf_op jit(solution)/shard_map/ppermute | solution.py:612
  20.7 4.8 %collective-permute-start.4 = (f32[40,2176]{1,0:T(8,128)S(1)}, f32[40,2176]{1,0:T(8,128)S(1)}, u32[]{:S(2)}, u32[]{:S(2)}) collective-permute-start(f32[40,2176]{1,0:T(8,128)S(1)} %get-tuple-element.44.halo), channel_id=1, source_target_pairs={{4,0},{1,5},{12,2},{3,13},{14,6},{7,15},{10,4},{5,11},{8,12},{13,9... | collective-permute-start | bytes 1044488 | tf_op jit(solution)/shard_map/ppermute | solution.py:612
  25.5 4.7 %tiles0.1 = (f32[1024,2048]{1,0:T(8,128)S(1)}, f32[32,2048]{1,0:T(8,128)S(1)}) custom-call(s32[4]{0:T(128)S(1)} %pad_add_fusion.place, f32[8,128]{1,0:T(8,128)S(1)} %get-tuple-element.43.own, f32[40,2176]{1,0:T(8,128)S(1)} %get-tuple-element.44.halo, f32[8,2048]{1,0:T(8,128)S(1)} %get-tuple-element.45.first, bf16[32,2048]{1,0:T(8,128)(2,1)S(1)} %get-tuple-element.46.right), custom_call_target="tpu_custom_call" | custom-call | tf_op jit(solution)/shard_map/tiles0/pallas_call | solution.py:341
  30.1 0.0 collective-permute-done.6.halo
  30.1 8.7 %tiles1.1 = (f32[2048,2048]{1,0:T(8,128)S(1)}, f32[32,2048]{1,0:T(8,128)S(1)}) custom-call(s32[4]{0:T(128)S(1)} %pad_add_fusion.place, f32[8,128]{1,0:T(8,128)S(1)} %get-tuple-element.43.own, f32[40,2176]{1,0:T(8,128)S(1)} %collective-permute-done.6.halo, f32[8,2048]{1,0:T(8,128)S(1)} %get-tuple-element.45.first, ...), custom_call_target="tpu_custom_call" | custom-call | tf_op jit(solution)/shard_map/tiles1/pallas_call | solution.py:389
  38.8 0.0 collective-permute-done.5.halo
  38.8 8.5 %tiles2.1 = (f32[2048,2048]{1,0:T(8,128)S(1)}, f32[32,2048]{1,0:T(8,128)S(1)}) custom-call(s32[4]{0:T(128)S(1)} %pad_add_fusion.place, f32[8,128]{1,0:T(8,128)S(1)} %get-tuple-element.43.own, f32[40,2176]{1,0:T(8,128)S(1)} %collective-permute-done.5.halo, f32[8,2048]{1,0:T(8,128)S(1)} %get-tuple-element.45.first, ...), custom_call_target="tpu_custom_call" | custom-call | tf_op jit(solution)/shard_map/tiles2/pallas_call | solution.py:389
  47.3 0.0 collective-permute-done.4.halo
  47.3 4.3 %tiles3.1 = (f32[7168,256]{1,0:T(8,128)S(1)}, f32[32,2048]{1,0:T(8,128)S(1)}) custom-call(s32[4]{0:T(128)S(1)} %pad_add_fusion.place, f32[8,128]{1,0:T(8,128)S(1)} %get-tuple-element.43.own, f32[40,2176]{1,0:T(8,128)S(1)} %collective-permute-done.4.halo, f32[8,2048]{1,0:T(8,128)S(1)} %get-tuple-element.45.first, ...), custom_call_target="tpu_custom_call" | custom-call | tf_op jit(solution)/shard_map/tiles3/pallas_call | solution.py:420
  51.6 0.0 collective-permute-start.7
  51.6 1.5 %collective-permute-done.7.other = f32[32,2048]{1,0:T(8,128)S(1)} collective-permute-done((f32[32,2048]{1,0:T(8,128)S(1)}, f32[32,2048]{1,0:T(8,128)S(1)}, u32[]{:S(2)}, u32[]{:S(2)}) %collective-permute-start.7) | collective-permute-done | bytes 262176 | tf_op jit(solution)/shard_map/ppermute | solution.py:617
  53.1 0.1 combine.1
  53.2 3.3 %collective-permute-start.10 = (f32[32,2048]{1,0:T(8,128)S(1)}, f32[32,2048]{1,0:T(8,128)S(1)}, u32[]{:S(2)}, u32[]{:S(2)}) collective-permute-start(f32[32,2048]{1,0:T(8,128)S(1)} %get-tuple-element.52.vector), channel_id=1, source_target_pairs={{2,0},{1,3},{6,2},{3,7},{4,6},{7,5},{12,4},{5,13},{14,12},{13,15},... | collective-permute-start | bytes 786440 | tf_op jit(solution)/shard_map/ppermute | solution.py:612
  56.5 5.0 %collective-permute-start.9 = (f32[32,2048]{1,0:T(8,128)S(1)}, f32[32,2048]{1,0:T(8,128)S(1)}, u32[]{:S(2)}, u32[]{:S(2)}) collective-permute-start(f32[32,2048]{1,0:T(8,128)S(1)} %get-tuple-element.52.vector), channel_id=1, source_target_pairs={{6,0},{1,7},{4,2},{3,5},{12,6},{7,13},{14,4},{5,15},{10,12},{13,11... | collective-permute-start | bytes 786440 | tf_op jit(solution)/shard_map/ppermute | solution.py:612
  61.5 5.4 %collective-permute-start.8 = (f32[32,2048]{1,0:T(8,128)S(1)}, f32[32,2048]{1,0:T(8,128)S(1)}, u32[]{:S(2)}, u32[]{:S(2)}) collective-permute-start(f32[32,2048]{1,0:T(8,128)S(1)} %get-tuple-element.52.vector), channel_id=1, source_target_pairs={{4,0},{1,5},{12,2},{3,13},{14,6},{7,15},{10,4},{5,11},{8,12},{13,9... | collective-permute-start | bytes 786440 | tf_op jit(solution)/shard_map/ppermute | solution.py:612
  66.9 1.7 %apply.3.before = f32[32,2048]{1,0:T(8,128)S(1)} custom-call(f32[32,2048]{1,0:T(8,128)S(1)} %get-tuple-element.52.vector, f32[1024,2048]{1,0:T(8,128)S(1)} %get-tuple-element.56.kept, f32[32,2048]{1,0:T(8,128)S(1)} %broadcast_in_dim.3.before), custom_call_target="tpu_custom_call" | custom-call | tf_op jit(solution)/shard_map/apply/pallas_call | solution.py:446
  68.6 0.0 collective-permute-done.10.vector
  68.6 3.3 %apply.4.before = f32[32,2048]{1,0:T(8,128)S(1)} custom-call(f32[32,2048]{1,0:T(8,128)S(1)} %collective-permute-done.10.vector, f32[2048,2048]{1,0:T(8,128)S(1)} %get-tuple-element.55.kept, f32[32,2048]{1,0:T(8,128)S(1)} %apply.3.before), custom_call_target="tpu_custom_call" | custom-call | tf_op jit(solution)/shard_map/apply/pallas_call | solution.py:446
  71.9 0.0 copy-start
  71.9 0.0 collective-permute-done.9.vector
  71.9 3.3 %apply.5.before = f32[32,2048]{1,0:T(8,128)S(1)} custom-call(f32[32,2048]{1,0:T(8,128)S(1)} %collective-permute-done.9.vector, f32[2048,2048]{1,0:T(8,128)S(1)} %get-tuple-element.54.kept, f32[32,2048]{1,0:T(8,128)S(1)} %apply.4.before), custom_call_target="tpu_custom_call" | custom-call | tf_op jit(solution)/shard_map/apply/pallas_call | solution.py:446
  75.2 0.0 collective-permute-done.8.vector
  75.2 1.6 %apply3.1.mine = f32[32,2048]{1,0:T(8,128)S(1)} custom-call(f32[32,2048]{1,0:T(8,128)S(1)} %collective-permute-done.8.vector, f32[7168,256]{1,0:T(8,128)S(1)} %get-tuple-element.53.kept, f32[32,2048]{1,0:T(8,128)S(1)} %apply.5.before), custom_call_target="tpu_custom_call" | custom-call | tf_op jit(solution)/shard_map/apply3/pallas_call | solution.py:471
  76.8 0.0 collective-permute-start.11
  76.8 1.5 %collective-permute-done.11.other = f32[32,2048]{1,0:T(8,128)S(1)} collective-permute-done((f32[32,2048]{1,0:T(8,128)S(1)}, f32[32,2048]{1,0:T(8,128)S(1)}, u32[]{:S(2)}, u32[]{:S(2)}) %collective-permute-start.11) | collective-permute-done | bytes 262176 | tf_op jit(solution)/shard_map/ppermute | solution.py:617
  78.3 0.8 finish.1
  79.1 0.7 collective-permute-start.12
  79.8 2.7 %collective-permute-start.13 = (f32[4,4224]{1,0:T(4,128)S(1)}, f32[4,4224]{1,0:T(4,128)S(1)}, u32[]{:S(2)}, u32[]{:S(2)}) collective-permute-start(f32[4,4224]{1,0:T(4,128)S(1)} %get-tuple-element.60), channel_id=1, source_target_pairs={{0,4},{1,5},{2,6},{3,7},{4,0},{5,1},{6,2},{7,3},{8,12},{9,13},{10,... | collective-permute-start | bytes 202760 | tf_op jit(solution)/shard_map/ppermute | solution.py:626
  82.5 1.2 %collective-permute-start.14 = (f32[4,4224]{1,0:T(4,128)S(1)}, f32[4,4224]{1,0:T(4,128)S(1)}, u32[]{:S(2)}, u32[]{:S(2)}) collective-permute-start(f32[4,4224]{1,0:T(4,128)S(1)} %get-tuple-element.61), channel_id=1, source_target_pairs={{0,6},{1,7},{2,0},{3,1},{4,2},{5,3},{6,4},{7,5},{8,14},{9,15},{10,... | collective-permute-start | bytes 202760 | tf_op jit(solution)/shard_map/ppermute | solution.py:626
  83.7 1.7 %collective-permute-done.12.behind1 = f32[4,4224]{1,0:T(4,128)S(1)} collective-permute-done((f32[4,4224]{1,0:T(4,128)S(1)}, f32[4,4224]{1,0:T(4,128)S(1)}, u32[]{:S(2)}, u32[]{:S(2)}) %collective-permute-start.12) | collective-permute-done | bytes 67616 | tf_op jit(solution)/shard_map/ppermute | solution.py:626
  85.4 0.7 collective-permute-done.13.behind2
  86.1 0.7 collective-permute-done.14.behind3
  86.8 20.7 %all_to_all.5.sums = f32[32,4,128]{2,1,0:T(4,128)S(1)} all-to-all(f32[32,4,128]{2,1,0:T(4,128)S(1)} %region_sums.1), channel_id=1, replica_groups=mesh['region'=32,'cols'=8] {'region'}, dimensions={0} | all-to-all | bytes 131072 | tf_op jit(solution)/shard_map/all_to_all | solution.py:675
  107.5 0.0 copy-done
  107.6 1.5 %result.1 = (f32[4,8192]{1,0:T(4,128)}, f32[4,8192]{1,0:T(4,128)}) custom-call(s32[4]{0:T(128)S(1)} %pad_add_fusion.place, f32[32,4,128]{2,1,0:T(4,128)S(1)} %all_to_all.5.sums, f32[4,8192]{1,0:T(4,128)S(1)} %copy-done, f32[4,4224]{1,0:T(4,128)S(1)} %get-tuple-element.58.own, f32[4,4224]{1,0:T(4,128)S(1)} %collective-permute-done.12.behind1, ...), custom_call_target="tpu_custom_call" | custom-call | tf_op jit(solution)/shard_map/result/pallas_call | solution.py:592
  (2 shorter events, 0.0 us)
Async XLA Ops:
  2.8 7.3 %collective-permute-start = (f32[4,2176]{1,0:T(4,128)S(1)}, f32[4,2176]{1,0:T(4,128)S(1)}, u32[]{:S(2)}, u32[]{:S(2)}) collective-permute-start(f32[4,2176]{1,0:T(4,128)S(1)} %get-tuple-element.33), channel_id=1, source_target_pairs={{0,2},{1,3},{2,4},{3,5},{4,6},{5,7},{6,0},{7,1},{8,10},{9,11},{10,... | collective-permute-start | bytes 104456 | tf_op jit(solution)/shard_map/ppermute | solution.py:626
  4.5 5.7 %collective-permute-start.1 = (f32[4,2176]{1,0:T(4,128)S(1)}, f32[4,2176]{1,0:T(4,128)S(1)}, u32[]{:S(2)}, u32[]{:S(2)}) collective-permute-start(f32[4,2176]{1,0:T(4,128)S(1)} %get-tuple-element.34), channel_id=1, source_target_pairs={{0,4},{1,5},{2,6},{3,7},{4,0},{5,1},{6,2},{7,3},{8,12},{9,13},{10,... | collective-permute-start | bytes 104456 | tf_op jit(solution)/shard_map/ppermute | solution.py:626
  7.4 3.9 %collective-permute-start.2 = (f32[4,2176]{1,0:T(4,128)S(1)}, f32[4,2176]{1,0:T(4,128)S(1)}, u32[]{:S(2)}, u32[]{:S(2)}) collective-permute-start(f32[4,2176]{1,0:T(4,128)S(1)} %get-tuple-element.35), channel_id=1, source_target_pairs={{0,6},{1,7},{2,0},{3,1},{4,2},{5,3},{6,4},{7,5},{8,14},{9,15},{10,... | collective-permute-start | bytes 104456 | tf_op jit(solution)/shard_map/ppermute | solution.py:626
  11.9 1.4 %collective-permute-start.3 = (f32[16,2176]{1,0:T(8,128)S(1)}, f32[16,2176]{1,0:T(8,128)S(1)}, u32[]{:S(2)}, u32[]{:S(2)}) collective-permute-start(f32[16,2176]{1,0:T(8,128)S(1)} %assemble.1.mine), channel_id=1, source_target_pairs={{0,1},{1,0},{2,3},{3,2},{4,5},{5,4},{6,7},{7,6},{8,9},{9,8},{10,11... | collective-permute-start | bytes 417800 | tf_op jit(solution)/shard_map/ppermute | solution.py:617
  14.3 15.9 %collective-permute-start.6 = (f32[40,2176]{1,0:T(8,128)S(1)}, f32[40,2176]{1,0:T(8,128)S(1)}, u32[]{:S(2)}, u32[]{:S(2)}) collective-permute-start(f32[40,2176]{1,0:T(8,128)S(1)} %get-tuple-element.44.halo), channel_id=1, source_target_pairs={{2,0},{1,3},{6,2},{3,7},{4,6},{7,5},{12,4},{5,13},{14,12},{13,15},... | collective-permute-start | bytes 1044488 | tf_op jit(solution)/shard_map/ppermute | solution.py:612
  16.4 22.4 %collective-permute-start.5 = (f32[40,2176]{1,0:T(8,128)S(1)}, f32[40,2176]{1,0:T(8,128)S(1)}, u32[]{:S(2)}, u32[]{:S(2)}) collective-permute-start(f32[40,2176]{1,0:T(8,128)S(1)} %get-tuple-element.44.halo), channel_id=1, source_target_pairs={{6,0},{1,7},{4,2},{3,5},{12,6},{7,13},{14,4},{5,15},{10,12},{13,11... | collective-permute-start | bytes 1044488 | tf_op jit(solution)/shard_map/ppermute | solution.py:612
  20.7 26.6 %collective-permute-start.4 = (f32[40,2176]{1,0:T(8,128)S(1)}, f32[40,2176]{1,0:T(8,128)S(1)}, u32[]{:S(2)}, u32[]{:S(2)}) collective-permute-start(f32[40,2176]{1,0:T(8,128)S(1)} %get-tuple-element.44.halo), channel_id=1, source_target_pairs={{4,0},{1,5},{12,2},{3,13},{14,6},{7,15},{10,4},{5,11},{8,12},{13,9... | collective-permute-start | bytes 1044488 | tf_op jit(solution)/shard_map/ppermute | solution.py:612
  51.6 1.6 %collective-permute-start.7 = (f32[32,2048]{1,0:T(8,128)S(1)}, f32[32,2048]{1,0:T(8,128)S(1)}, u32[]{:S(2)}, u32[]{:S(2)}) collective-permute-start(f32[32,2048]{1,0:T(8,128)S(1)} %get-tuple-element.50.mine), channel_id=1, source_target_pairs={{0,1},{1,0},{2,3},{3,2},{4,5},{5,4},{6,7},{7,6},{8,9},{9,8},{10,11... | collective-permute-start | bytes 786440 | tf_op jit(solution)/shard_map/ppermute | solution.py:617
  53.2 15.4 %collective-permute-start.10 = (f32[32,2048]{1,0:T(8,128)S(1)}, f32[32,2048]{1,0:T(8,128)S(1)}, u32[]{:S(2)}, u32[]{:S(2)}) collective-permute-start(f32[32,2048]{1,0:T(8,128)S(1)} %get-tuple-element.52.vector), channel_id=1, source_target_pairs={{2,0},{1,3},{6,2},{3,7},{4,6},{7,5},{12,4},{5,13},{14,12},{13,15},... | collective-permute-start | bytes 786440 | tf_op jit(solution)/shard_map/ppermute | solution.py:612
  56.5 15.4 %collective-permute-start.9 = (f32[32,2048]{1,0:T(8,128)S(1)}, f32[32,2048]{1,0:T(8,128)S(1)}, u32[]{:S(2)}, u32[]{:S(2)}) collective-permute-start(f32[32,2048]{1,0:T(8,128)S(1)} %get-tuple-element.52.vector), channel_id=1, source_target_pairs={{6,0},{1,7},{4,2},{3,5},{12,6},{7,13},{14,4},{5,15},{10,12},{13,11... | collective-permute-start | bytes 786440 | tf_op jit(solution)/shard_map/ppermute | solution.py:612
  61.5 13.7 %collective-permute-start.8 = (f32[32,2048]{1,0:T(8,128)S(1)}, f32[32,2048]{1,0:T(8,128)S(1)}, u32[]{:S(2)}, u32[]{:S(2)}) collective-permute-start(f32[32,2048]{1,0:T(8,128)S(1)} %get-tuple-element.52.vector), channel_id=1, source_target_pairs={{4,0},{1,5},{12,2},{3,13},{14,6},{7,15},{10,4},{5,11},{8,12},{13,9... | collective-permute-start | bytes 786440 | tf_op jit(solution)/shard_map/ppermute | solution.py:612
  71.9 35.7 %copy-start = (f32[4,8192]{1,0:T(4,128)S(1)}, f32[4,8192]{1,0:T(4,128)}, u32[]{:S(2)}) copy-start(f32[4,8192]{1,0:T(4,128)} %innovations.3) | copy-start | bytes 393220
  76.8 1.6 %collective-permute-start.11 = (f32[32,2048]{1,0:T(8,128)S(1)}, f32[32,2048]{1,0:T(8,128)S(1)}, u32[]{:S(2)}, u32[]{:S(2)}) collective-permute-start(f32[32,2048]{1,0:T(8,128)S(1)} %apply3.1.mine), channel_id=1, source_target_pairs={{0,1},{1,0},{2,3},{3,2},{4,5},{5,4},{6,7},{7,6},{8,9},{9,8},{10,11... | collective-permute-start | bytes 786440 | tf_op jit(solution)/shard_map/ppermute | solution.py:617
  79.1 6.3 %collective-permute-start.12 = (f32[4,4224]{1,0:T(4,128)S(1)}, f32[4,4224]{1,0:T(4,128)S(1)}, u32[]{:S(2)}, u32[]{:S(2)}) collective-permute-start(f32[4,4224]{1,0:T(4,128)S(1)} %get-tuple-element.59), channel_id=1, source_target_pairs={{0,2},{1,3},{2,4},{3,5},{4,6},{5,7},{6,0},{7,1},{8,10},{9,11},{10,... | collective-permute-start | bytes 202760 | tf_op jit(solution)/shard_map/ppermute | solution.py:626
  79.8 6.3 %collective-permute-start.13 = (f32[4,4224]{1,0:T(4,128)S(1)}, f32[4,4224]{1,0:T(4,128)S(1)}, u32[]{:S(2)}, u32[]{:S(2)}) collective-permute-start(f32[4,4224]{1,0:T(4,128)S(1)} %get-tuple-element.60), channel_id=1, source_target_pairs={{0,4},{1,5},{2,6},{3,7},{4,0},{5,1},{6,2},{7,3},{8,12},{9,13},{10,... | collective-permute-start | bytes 202760 | tf_op jit(solution)/shard_map/ppermute | solution.py:626
  82.5 4.3 %collective-permute-start.14 = (f32[4,4224]{1,0:T(4,128)S(1)}, f32[4,4224]{1,0:T(4,128)S(1)}, u32[]{:S(2)}, u32[]{:S(2)}) collective-permute-start(f32[4,4224]{1,0:T(4,128)S(1)} %get-tuple-element.61), channel_id=1, source_target_pairs={{0,6},{1,7},{2,0},{3,1},{4,2},{5,3},{6,4},{7,5},{8,14},{9,15},{10,... | collective-permute-start | bytes 202760 | tf_op jit(solution)/shard_map/ppermute | solution.py:626
